TPU v7x, 256 devices: a whole 4x4x8 slice. The times are simulated.
256 devices in a mesh: row: 128 (over z, y_lo, x, core), col: 2 (over y_hi).
Axes of the slice: x: 4, y: 4 (y_hi: 2, y_lo: 2; y = y_hi * 2 + y_lo), z: 8, core: 2. Of those that a mesh axis runs over, the one named last changes fastest.
Arguments:
- matrix_panel: bfloat16 [128, 1048576], P('col', 'row'), may hold values from -6 to 6
- row_signs: int32 [1048576], P('row'), may hold values from -1 to 1, as said below
- sample_rows: int32 [16384], replicated, may hold values from 0 to 1048575, as said below
Outputs:
- sketch: float32 [128, 16384], P('col', 'row')
- gram: float32 [128, 128], P('col')
Inputs may be any that keep to these rules, and one draw needn't show every extreme that they name: `row_signs`: each entry is -1 or +1. `sample_rows`: strictly increasing, so all distinct.
All inputs are finite; a program needn't handle non-finite values.
Results may differ from a plain program's by a relative error of at most 0.0003.
Values sent between devices are 32-bit elements; how exact they have to be, the bound alone decides.
A program may use at most 64 MiB of HBM per device.

v0:
```python
import jax
import jax.numpy as jnp
from jax import lax
from jax.sharding import PartitionSpec as P


def parity_sign(left, right, bit_count):
    common = jnp.bitwise_and(left, right)
    total = jnp.zeros_like(common)
    for bit_index in range(bit_count):
        total = total + jnp.bitwise_and(jnp.right_shift(common, bit_index), 1)
    return (1 - 2 * jnp.bitwise_and(total, 1)).astype(jnp.float32)


def hadamard(order_size):
    bit_count = order_size.bit_length() - 1
    row_index = jnp.arange(order_size, dtype=jnp.int32)
    return parity_sign(row_index[:, None], row_index[None, :], bit_count)


def local_mix(block, signs):
    columns, length = block.shape
    first_size = min(length, 256)
    second_size = length // first_size
    values = block.astype(jnp.float32) * signs.astype(jnp.float32)[None, :]
    values = values.reshape(columns, first_size, second_size)
    values = jnp.einsum(
        "cab,ad->cdb", values, hadamard(first_size), precision=lax.Precision.HIGHEST
    )
    values = jnp.einsum(
        "cdb,be->cde", values, hadamard(second_size), precision=lax.Precision.HIGHEST
    )
    return values.reshape(columns, length) / jnp.sqrt(jnp.float32(length))


def body(matrix_panel, row_signs, sample_rows):
    devices = lax.axis_size("row")
    position = lax.axis_index("row")
    bit_count = devices.bit_length() - 1
    columns, length = matrix_panel.shape
    everything = sample_rows.shape[0]
    mixed = local_mix(matrix_panel, row_signs)
    owner = sample_rows // length
    offset = sample_rows - owner * length
    chosen = jnp.take(mixed, offset, axis=1)
    weights = parity_sign(owner, position, bit_count)
    summed = lax.psum_scatter(chosen * weights[None, :], "row", scatter_dimension=1, tiled=True)
    sketch = summed / jnp.sqrt(jnp.float32(devices))
    gathered = lax.all_gather(sketch, "col", axis=0, tiled=True)
    partial_gram = jnp.dot(gathered, gathered.T, precision=lax.Precision.HIGHEST)
    totals = lax.psum(partial_gram, "row")
    own_rows = lax.dynamic_slice_in_dim(totals, lax.axis_index("col") * columns, columns, 0)
    gram = own_rows / everything
    return (sketch, gram)


def solution(mesh):
    return jax.shard_map(
        body,
        mesh=mesh,
        in_specs=(P("col", "row"), P("row"), P()),
        out_specs=(P("col", "row"), P("col", None)),
        check_vma=False,
    )
```

profile of v0, /device:TPU:1, one launch (start us, length us, event | category | flops | bytes accessed | tf_op | source)
XLA Modules:
  0.0 1610.4 jit_solution(2291911694017970471)
XLA Ops:
  7.2 0.0 reduce-scatter.2.cloned.1.call-start
  7.2 0.9 compare_and_fusion
  8.1 1.0 subtract_convert_fusion
  9.1 0.8 convert_element_type.17
  9.8 1.4 convert_multiply_fusion
  11.3 2.7 copy.9
  14.0 4.5 copy.10
  18.4 2.2 fusion
  20.6 1.9 convolution_multiply_fusion
  22.5 4.5 copy.11
  27.0 56.9 %gather_fusion = f32[16384,64]{1,0:T(8,128)} fusion(f32[64,8192]{0,1:T(8,128)} %bitcast.17, s32[16384]{0:T(1024)S(1)} %get-tuple-element.9), kind=kCustom, calls=%fused_computation | custom fusion | bytes 8454144 | tf_op jit(solution)/shard_map/jit(_take)/gather | solution.py:45
  83.9 7.6 multiply_bitcast_fusion
  91.5 0.0 reduce-scatter.2.cloned.1.call-update
  91.5 0.0 all-reduce.2.cloned.1.call-start
  91.6 574.3 %reduce-scatter.2.cloned.1.call-done = f32[64,128]{0,1:T(8,128)} async-done(((f32[64,16384]{0,1:T(8,128)}), f32[64,128]{0,1:T(8,128)}) %reduce-scatter.2.cloned.1.call-update) | async-done | bytes 32784 | tf_op jit(solution)/shard_map/reduce_scatter | solution.py:47
  665.9 0.8 broadcast_multiply_fusion
  666.7 0.1 copy.13
  666.8 0.0 copy-start
  666.8 4.9 all_gather.3
  671.8 0.9 fusion.81
  672.7 0.0 all-reduce.2.cloned.1.call-update
  672.7 929.5 %all-reduce.2.cloned.1.call-done = f32[128,128]{1,0:T(8,128)} async-done(((f32[128,128]{1,0:T(8,128)}), f32[128,128]{1,0:T(8,128)}) %all-reduce.2.cloned.1.call-update) | async-done | bytes 65552 | tf_op jit(solution)/shard_map/psum | solution.py:51
  1602.2 1.4 dynamic-slice_multiply_fusion
  1603.6 0.0 copy-done
Async XLA Ops:
  7.2 658.7 %reduce-scatter.2.cloned.1.call-start = ((), (), s32[]{:S(2)}) async-start(), calls=%async_computation.1 | async-start | bytes 8454144 | tf_op jit(solution)/shard_map/reduce_scatter | solution.py:47
  91.5 1510.7 %all-reduce.2.cloned.1.call-start = ((), (), s32[]{:S(2)}) async-start(), calls=%async_computation.2 | async-start | bytes 131072 | tf_op jit(solution)/shard_map/psum | solution.py:51
  666.8 936.8 %copy-start = (f32[64,128]{1,0:T(8,128)}, f32[64,128]{1,0:T(8,128)S(1)}, u32[]{:S(2)}) copy-start(f32[64,128]{1,0:T(8,128)S(1)} %copy.13) | copy-start | bytes 98308
Sparse Core Ops, SparseCore 0:
  91.6 574.2 reduce-scatter.1
  672.8 929.3 all-reduce.1
where the time goes:
time: 1610 us
  waiting for transfers between devices  1500 us (93%)
  local copies, waits for them, and re-layouts  68.7 us (4%)
    psum x1, waiting for transfers between devices, body(): totals = lax.psum(partial_gram, 'row')  929 us
    reduce_scatter x1, waiting for transfers between devices, body(): lax.psum_scatter(chosen * weights[None, :], 'row', scatter_dimension=1, t...  574 us
    gather x1, local copies, waits for them, and re-layouts, body(): chosen = jnp.take(mixed, offset, axis=1)  56.9 us
  transfers between devices with their start and end apart: 2, of which 2 were waited for; matrix products, arithmetic and copies ran while one was open for 0% of the time, Pallas kernels for 0%

commit v1 on v0

v1 whole, which is shorter than its diff:
```python
import functools

import jax
import jax.numpy as jnp
from jax import lax
from jax.experimental import pallas as pl
from jax.experimental.pallas import tpu as pltpu
from jax.sharding import PartitionSpec as P

MESH = pl.DeviceIdType.MESH
Z = 8
PLANE = 8
CORES = 2
BLOCK = 128
COLS = 64
SPLIT = 4
DEPTH = 2048
CHUNK = PLANE * CORES * BLOCK


def parity(value, shift):
    while shift:
        value = value ^ (value >> shift)
        shift //= 2
    return value & 1


def sign_of(odd):
    return (1 - 2 * odd).astype(jnp.float32)


def mixed_chunk(position, rows, x_ref):
    count = rows.shape[1]
    bit = lambda k: sign_of((rows >> k) & 1)
    wide = lambda k: jnp.broadcast_to(bit(k), (16, count)).astype(jnp.bfloat16)
    spread = jnp.broadcast_to(rows, (16, count))
    low = parity(spread & lax.broadcasted_iota(jnp.int32, (16, count), 0), 2)
    tiles = [sign_of(low).astype(jnp.bfloat16)]
    for k in range(4, 8):
        flip = wide(k)
        tiles = tiles + [tile * flip for tile in tiles]
    upper = [None]
    for k in range(8, 11):
        flip = wide(k)
        upper = upper + [flip if one is None else one * flip for one in upper]
    total = jnp.zeros((SPLIT * COLS, count), jnp.float32)
    for k, flip in enumerate(upper):
        signs = jnp.concatenate([tile if flip is None else tile * flip for tile in tiles], axis=0)
        total = total + jnp.dot(
            x_ref[:, k * 256:(k + 1) * 256], signs, preferred_element_type=jnp.float32
        )
    parts = [total[a * COLS:(a + 1) * COLS] for a in range(SPLIT)]
    for k in (11, 12):
        flip = bit(k)
        parts = [parts[2 * i] + flip * parts[2 * i + 1] for i in range(len(parts) // 2)]
    weight = sign_of(parity((rows >> 13) & position, 4)) * (1.0 / 1024.0)
    return parts[0] * weight


def kernel(
    x_ref, sign_ref, rows_ref, sketch_ref, gram_ref,
    xs, part, got_core, summed, got_plane, send_z, got_z, both, gram_part, got_rs, totals, pieces,
    core_send, core_recv, plane_send, plane_recv, z_send, z_recv,
    col_sem, rs_send, rs_recv, tot_send, tot_recv, out_send, out_recv,
):
    position = lax.axis_index("row")
    col = lax.axis_index("col")
    z = position // 16
    mine = (position // 2) % 8
    core = position % 2

    def device(z_at, plane_at, core_at):
        return (z_at * 16 + plane_at * 2 + core_at, col)

    def z_core(k):
        other = (z * 2 + core + k) % 16
        return other, device(other // 2, mine, other % 2)

    barrier = pltpu.get_barrier_semaphore()
    for d in range(1, PLANE):
        pl.semaphore_signal(barrier, inc=1, device_id=device(z, mine ^ d, core), device_id_type=MESH)
    for k in range(1, 16):
        pl.semaphore_signal(barrier, inc=1, device_id=z_core(k)[1], device_id_type=MESH)
    pl.semaphore_signal(barrier, inc=1, device_id=(position, 1 - col), device_id_type=MESH)

    for a in range(SPLIT):
        window = slice(a * DEPTH, (a + 1) * DEPTH)
        xs[a * COLS:(a + 1) * COLS, :] = (
            x_ref[:, window].astype(jnp.float32) * sign_ref[:, window].astype(jnp.float32)
        ).astype(jnp.bfloat16)

    pl.semaphore_wait(barrier, 23)

    def target(t):
        return (z + jnp.where(t % 2 == 0, 4 + t // 2, 4 - (t + 1) // 2)) % Z

    def core_copy(t):
        return pltpu.make_async_remote_copy(
            src_ref=part.at[t, 1 - core], dst_ref=got_core.at[t],
            send_sem=core_send.at[t], recv_sem=core_recv.at[t],
            device_id=device(z, mine, 1 - core), device_id_type=MESH,
        )

    def plane_copy(t, d):
        return pltpu.make_async_remote_copy(
            src_ref=summed.at[t, mine ^ d], dst_ref=got_plane.at[t, d - 1],
            send_sem=plane_send.at[t, d - 1], recv_sem=plane_recv.at[t, d - 1],
            device_id=device(z, mine ^ d, core), device_id_type=MESH,
        )

    def z_copy(t):
        return pltpu.make_async_remote_copy(
            src_ref=send_z.at[t], dst_ref=got_z.at[t],
            send_sem=z_send.at[t], recv_sem=z_recv.at[t],
            device_id=device(target(t), mine, core), device_id_type=MESH,
        )

    def compute(t):
        start = pl.multiple_of(target(t) * CHUNK, CHUNK)
        chunk = mixed_chunk(position, rows_ref[:, pl.ds(start, CHUNK)], xs)
        for j in range(16):
            part[t, j % 2, j // 2] = chunk[:, j * BLOCK:(j + 1) * BLOCK]
        core_copy(t).start()

    def plane_stage(t):
        core_copy(t).wait_recv()
        summed[t] = part[t, core] + got_core[t]
        for d in range(1, PLANE):
            plane_copy(t, d).start()

    def z_stage(t):
        for d in range(1, PLANE):
            plane_copy(t, d).wait_recv()
        block = summed[t, mine]
        for d in range(1, PLANE):
            block = block + got_plane[t, d - 1]
        send_z[t] = block

    def step(t, carry):
        @pl.when(t < Z)
        def _():
            compute(t)

        @pl.when((t >= 1) & (t <= Z))
        def _():
            plane_stage(t - 1)

        @pl.when(t >= 2)
        def _():
            z_stage(t - 2)

        @pl.when((t >= 2) & (t <= Z))
        def _():
            z_copy(t - 2).start()

        return carry

    lax.fori_loop(0, Z + 2, step, 0)

    own = send_z[Z - 1]
    for t in range(Z - 1):
        z_copy(t).wait_recv()
        own = own + got_z[t]
    sketch_ref[...] = own

    place = pl.ds(pl.multiple_of(col * COLS, COLS), COLS)
    both[place, :] = own
    col_copy = pltpu.make_async_remote_copy(
        src_ref=both.at[place], dst_ref=both.at[place],
        send_sem=col_sem.at[0], recv_sem=col_sem.at[1],
        device_id=(position, 1 - col), device_id_type=MESH,
    )
    col_copy.start()
    other = pl.ds(pl.multiple_of((1 - col) * COLS, COLS), COLS)
    pltpu.make_async_remote_copy(
        src_ref=both.at[other], dst_ref=both.at[other],
        send_sem=col_sem.at[0], recv_sem=col_sem.at[1],
        device_id=(position, 1 - col), device_id_type=MESH,
    ).wait_recv()
    gram_part[...] = lax.dot_general(
        own, both[...], (((1,), (1,)), ((), ())),
        precision=lax.Precision.HIGHEST, preferred_element_type=jnp.float32,
    ).reshape(PLANE, 8, 128)

    def rs_copy(d):
        return pltpu.make_async_remote_copy(
            src_ref=gram_part.at[mine ^ d], dst_ref=got_rs.at[d - 1],
            send_sem=rs_send.at[d - 1], recv_sem=rs_recv.at[d - 1],
            device_id=device(z, mine ^ d, core), device_id_type=MESH,
        )

    for d in range(1, PLANE):
        rs_copy(d).start()
    for d in range(1, PLANE):
        rs_copy(d).wait_recv()
    piece = gram_part[mine]
    for d in range(1, PLANE):
        piece = piece + got_rs[d - 1]
    me = z * 2 + core
    totals[me] = piece

    def tot_copy(k, to):
        return pltpu.make_async_remote_copy(
            src_ref=totals.at[me], dst_ref=totals.at[me],
            send_sem=tot_send.at[k - 1], recv_sem=tot_recv.at[k - 1],
            device_id=to, device_id_type=MESH,
        )

    for k in range(1, 16):
        tot_copy(k, z_core(k)[1]).start()
    for k in range(1, 16):
        sender = (me + 16 - k) % 16
        pltpu.make_async_remote_copy(
            src_ref=totals.at[sender], dst_ref=totals.at[sender],
            send_sem=tot_send.at[k - 1], recv_sem=tot_recv.at[k - 1],
            device_id=z_core(k)[1], device_id_type=MESH,
        ).wait_recv()
    piece = totals[0]
    for k in range(1, 16):
        piece = piece + totals[k]
    pieces[mine] = piece * (1.0 / 16384.0)

    def out_copy(d, at):
        return pltpu.make_async_remote_copy(
            src_ref=pieces.at[at], dst_ref=pieces.at[at],
            send_sem=out_send.at[d - 1], recv_sem=out_recv.at[d - 1],
            device_id=device(z, mine ^ d, core), device_id_type=MESH,
        )

    for d in range(1, PLANE):
        out_copy(d, mine).start()
    for d in range(1, PLANE):
        out_copy(d, mine ^ d).wait_recv()
    gram_ref[...] = pieces[...].reshape(COLS, 128)

    def drain(t, carry):
        core_copy(t).wait_send()
        for d in range(1, PLANE):
            plane_copy(t, d).wait_send()

        @pl.when(t < Z - 1)
        def _():
            z_copy(t).wait_send()

        return carry

    lax.fori_loop(0, Z, drain, 0)
    col_copy.wait_send()
    for d in range(1, PLANE):
        rs_copy(d).wait_send()
        out_copy(d, mine).wait_send()
    for k in range(1, 16):
        tot_copy(k, z_core(k)[1]).wait_send()


def body(matrix_panel, row_signs, sample_rows):
    vmem = pl.BlockSpec(memory_space=pltpu.VMEM)
    f32 = jnp.float32
    block = (COLS, BLOCK)
    sems = pltpu.SemaphoreType.DMA
    return pl.pallas_call(
        kernel,
        out_shape=(jax.ShapeDtypeStruct(block, f32), jax.ShapeDtypeStruct(block, f32)),
        in_specs=[vmem] * 3,
        out_specs=(vmem, vmem),
        scratch_shapes=[
            pltpu.VMEM((SPLIT * COLS, DEPTH), jnp.bfloat16),
            pltpu.VMEM((Z, CORES, PLANE) + block, f32),
            pltpu.VMEM((Z, PLANE) + block, f32),
            pltpu.VMEM((Z, PLANE) + block, f32),
            pltpu.VMEM((Z, PLANE - 1) + block, f32),
            pltpu.VMEM((Z,) + block, f32),
            pltpu.VMEM((Z - 1,) + block, f32),
            pltpu.VMEM((2 * COLS, BLOCK), f32),
            pltpu.VMEM((PLANE, 8, 128), f32),
            pltpu.VMEM((PLANE - 1, 8, 128), f32),
            pltpu.VMEM((16, 8, 128), f32),
            pltpu.VMEM((PLANE, 8, 128), f32),
            sems((Z,)), sems((Z,)),
            sems((Z, PLANE - 1)), sems((Z, PLANE - 1)),
            sems((Z - 1,)), sems((Z - 1,)),
            sems((2,)),
            sems((PLANE - 1,)), sems((PLANE - 1,)),
            sems((15,)), sems((15,)),
            sems((PLANE - 1,)), sems((PLANE - 1,)),
        ],
        compiler_params=pltpu.CompilerParams(
            collective_id=0, has_side_effects=True, vmem_limit_bytes=56 * 2**20
        ),
        cost_estimate=pl.CostEstimate(
            flops=2 * COLS * 8192 * 16384, bytes_accessed=2**21, transcendentals=0
        ),
    )(matrix_panel, row_signs.reshape(1, -1), sample_rows.reshape(1, -1))


def solution(mesh):
    return jax.shard_map(
        body,
        mesh=mesh,
        in_specs=(P("col", "row"), P("row"), P()),
        out_specs=(P("col", "row"), P("col", None)),
        check_vma=False,
    )
```

time: 1610 us -> 71.6 us (0.04)
  waiting for transfers between devices: 1500 us -> 0 us
  Pallas kernels: 0 us -> 68.8 us
  local copies, waits for them, and re-layouts: 68.7 us -> 2 us
    psum x1 -> x0, waiting for transfers between devices: 929 us -> none  [body(): totals = lax.psum(partial_gram, 'row')]
    reduce_scatter x1 -> x0, waiting for transfers between devices: 574 us -> none  [body(): lax.psum_scatter(chosen * weights[None, :], 'row', scatter_dimension=1, t...]
    pallas_call x0 -> x1, Pallas kernels: none -> 68.8 us  [body(): pl.pallas_call(kernel, out_shape=(jax.ShapeDtypeStruct(block, f32), jax.S...]
    gather x1 -> x0, local copies, waits for them, and re-layouts: 56.9 us -> none  [body(): chosen = jnp.take(mixed, offset, axis=1)]
  transfers between devices with their start and end apart: 2 -> 0, of which waited for: 2 -> 0; matrix products, arithmetic and copies ran while one was open for 0% -> 0% of each run, Pallas kernels for 0% -> 0%
where the time goes in v1:
time: 71.6 us; the launch traced here: 71.4 us
  Pallas kernels  68.8 us (96%)
  local copies, waits for them, and re-layouts  2 us (3%)
    pallas_call x1, Pallas kernels, body(): pl.pallas_call(kernel, out_shape=(jax.ShapeDtypeStruct(block, f32), jax.S...  68.8 us
    unnamed x4, local copies, waits for them, and re-layouts  2 us

profile of v1, /device:TPU:1, one launch (start us, length us, event | category | flops | bytes accessed | tf_op | source)
XLA Modules:
  0.0 71.4 jit_solution(2999631995041596464)
XLA Ops:
  0.6 68.8 %shard_map.50 = (f32[64,128]{1,0:T(8,128)}, f32[64,128]{1,0:T(8,128)}) custom-call(bf16[64,8192]{1,0:T(8,128)(2,1)} %x_ref.1, s32[1,8192]{1,0:T(1,128)} %bitcast.3, s32[1,16384]{1,0:T(1,128)} %bitcast.2), custom_call_target="tpu_custom_call" | custom-call | flops 17179869184 | bytes 2097152 | tf_op jit(solution)/shard_map/pallas_call | solution.py:261
  69.4 0.0 copy-start
  69.5 1.4 %copy.7 = f32[64,128]{1,0:T(8,128)} copy(f32[64,128]{1,0:T(8,128)} %get-tuple-element.4) | data formatting | bytes 65536
  70.8 0.0 copy-done
  70.8 0.6 copy.8
Async XLA Ops:
  69.4 1.4 %copy-start = (f32[64,128]{1,0:T(8,128)S(1)}, f32[64,128]{1,0:T(8,128)}, u32[]{:S(2)}) copy-start(f32[64,128]{1,0:T(8,128)} %get-tuple-element.5) | copy-start | bytes 98308

commit v2 on v1

v2 whole, which is shorter than its diff:
```python
import functools

import jax
import jax.numpy as jnp
from jax import lax
from jax.experimental import pallas as pl
from jax.experimental.pallas import tpu as pltpu
from jax.sharding import PartitionSpec as P

MESH = pl.DeviceIdType.MESH
Z = 8
PLANE = 8
CORES = 2
BLOCK = 128
COLS = 64
SPLIT = 4
DEPTH = 2048
CHUNK = PLANE * CORES * BLOCK
HOLD = 2


def parity(value, shift):
    while shift:
        value = value ^ (value >> shift)
        shift //= 2
    return value & 1


def sign_of(odd):
    return (1 - 2 * odd).astype(jnp.float32)


def mixed_chunk(position, rows, x_ref):
    count = rows.shape[1]
    bit = lambda k: sign_of((rows >> k) & 1)
    wide = lambda k: jnp.broadcast_to(bit(k), (16, count)).astype(jnp.bfloat16)
    spread = jnp.broadcast_to(rows, (16, count))
    low = parity(spread & lax.broadcasted_iota(jnp.int32, (16, count), 0), 2)
    tiles = [sign_of(low).astype(jnp.bfloat16)]
    for k in range(4, 8):
        flip = wide(k)
        tiles = tiles + [tile * flip for tile in tiles]
    upper = [None]
    for k in range(8, 11):
        flip = wide(k)
        upper = upper + [flip if one is None else one * flip for one in upper]
    total = jnp.zeros((SPLIT * COLS, count), jnp.float32)
    for k, flip in enumerate(upper):
        signs = jnp.concatenate([tile if flip is None else tile * flip for tile in tiles], axis=0)
        total = total + jnp.dot(
            x_ref[:, k * 256:(k + 1) * 256], signs, preferred_element_type=jnp.float32
        )
    parts = [total[a * COLS:(a + 1) * COLS] for a in range(SPLIT)]
    for k in (11, 12):
        flip = bit(k)
        parts = [parts[2 * i] + flip * parts[2 * i + 1] for i in range(len(parts) // 2)]
    weight = sign_of(parity((rows >> 13) & position, 4)) * (1.0 / 1024.0)
    return parts[0] * weight


def kernel(
    x_ref, sign_ref, rows_ref, sketch_ref, gram_ref,
    xs, part, got_core, summed, got_first, middle, got_second, got_plane, send_z, got_z,
    both, gram_part, got_rs, totals, pieces,
    core_send, core_recv, first_send, first_recv, second_send, second_recv,
    plane_send, plane_recv, z_send, z_recv,
    col_sem, rs_send, rs_recv, tot_send, tot_recv, out_send, out_recv,
):
    position = lax.axis_index("row")
    col = lax.axis_index("col")
    z = position // 16
    y = (position // 8) % 2
    x = (position // 2) % 4
    core = position % 2
    mine = y * 4 + x

    def device(z_at=z, y_at=y, x_at=x, core_at=core):
        return (((z_at * 2 + y_at) * 4 + x_at) * 2 + core_at, col)

    def in_plane(d):
        return device(y_at=y ^ (d // 4), x_at=x ^ (d % 4))

    def in_line(d):
        return device(x_at=x ^ (d // 2), core_at=core ^ (d % 2))

    def across(k):
        other = (z * 2 + y + k) % 16
        return device(z_at=other // 2, y_at=other % 2)

    partner = (position, 1 - col)

    barrier = pltpu.get_barrier_semaphore()
    known = [in_plane(d) for d in range(1, 8)]
    known += [in_line(d) for d in (1, 3, 5, 7)]
    known += [device(z_at=(z + k) % Z, y_at=y ^ d) for k in range(1, Z) for d in range(2)]
    known += [partner]
    for to in known:
        pl.semaphore_signal(barrier, inc=1, device_id=to, device_id_type=MESH)

    for a in range(SPLIT):
        window = slice(a * DEPTH, (a + 1) * DEPTH)
        xs[a * COLS:(a + 1) * COLS, :] = (
            x_ref[:, window].astype(jnp.float32) * sign_ref[:, window].astype(jnp.float32)
        ).astype(jnp.bfloat16)

    def copy(src, dst, send, recv, to):
        return pltpu.make_async_remote_copy(
            src_ref=src, dst_ref=dst, send_sem=send, recv_sem=recv,
            device_id=to, device_id_type=MESH,
        )

    def target(t):
        return (z + jnp.where(t % 2 == 0, 4 + t // 2, 4 - (t + 1) // 2)) % Z

    def core_copy(t):
        return copy(
            part.at[t, 1 - core], got_core.at[t], core_send.at[t], core_recv.at[t],
            device(core_at=1 - core),
        )

    def x_first(t, d):
        return copy(
            summed.at[t, pl.ds(2 * (x ^ d), 2)], got_first.at[t, pl.ds(2 * (d - 1), 2)],
            first_send.at[t, d - 1], first_recv.at[t, d - 1], device(x_at=x ^ d),
        )

    def y_second(t):
        return copy(
            middle.at[t, 1 - y], got_second.at[t, 0],
            second_send.at[t, 0], second_recv.at[t, 0], device(y_at=1 - y),
        )

    def y_first(t):
        return copy(
            summed.at[t, pl.ds(4 * (1 - y), 4)], got_first.at[t, pl.ds(0, 4)],
            first_send.at[t, 0], first_recv.at[t, 0], device(y_at=1 - y),
        )

    def x_second(t, d):
        return copy(
            middle.at[t, x ^ d], got_second.at[t, d - 1],
            second_send.at[t, d - 1], second_recv.at[t, d - 1], device(x_at=x ^ d),
        )

    def plane_copy(d):
        return copy(
            summed.at[Z - 1, mine ^ d], got_plane.at[d - 1],
            plane_send.at[d - 1], plane_recv.at[d - 1], in_plane(d),
        )

    def z_copy(t):
        return copy(
            send_z.at[t], got_z.at[t], z_send.at[t], z_recv.at[t], device(z_at=target(t))
        )

    def first_stage(t):
        core_copy(t).wait_recv()

        @pl.when(core == 0)
        def _():
            for j in range(PLANE):
                summed[t, (j % 4) * 2 + j // 4] = part[t, 0, j] + got_core[t, j]
            for d in (2, 1, 3):
                x_first(t, d).start()

        @pl.when(core == 1)
        def _():
            for j in range(PLANE):
                summed[t, j] = part[t, 1, j] + got_core[t, j]
            y_first(t).start()

    def second_stage(t):
        @pl.when(core == 0)
        def _():
            for d in range(1, 4):
                x_first(t, d).wait_recv()
            for j in range(2):
                middle[t, j] = (
                    (summed[t, 2 * x + j] + got_first[t, j])
                    + (got_first[t, 2 + j] + got_first[t, 4 + j])
                )
            y_second(t).start()

        @pl.when(core == 1)
        def _():
            y_first(t).wait_recv()
            for j in range(4):
                middle[t, j] = summed[t, 4 * y + j] + got_first[t, j]
            for d in (2, 1, 3):
                x_second(t, d).start()

    def third_stage(t):
        @pl.when(core == 0)
        def _():
            y_second(t).wait_recv()
            send_z[t] = middle[t, y] + got_second[t, 0]

        @pl.when(core == 1)
        def _():
            for d in range(1, 4):
                x_second(t, d).wait_recv()
            send_z[t] = (middle[t, x] + got_second[t, 0]) + (got_second[t, 1] + got_second[t, 2])

        z_copy(t).start()

    def step(t, carry):
        start = pl.multiple_of(target(t) * CHUNK, CHUNK)
        chunk = mixed_chunk(position, rows_ref[:, pl.ds(start, CHUNK)], xs)
        for j in range(16):
            part[t, j % 2, j // 2] = chunk[:, j * BLOCK:(j + 1) * BLOCK]

        @pl.when(t == HOLD - 1)
        def _():
            pl.semaphore_wait(barrier, len(known))
            for k in range(HOLD):
                core_copy(k).start()

        @pl.when(t >= HOLD)
        def _():
            core_copy(t).start()

        @pl.when(t == HOLD)
        def _():
            for k in range(HOLD):
                first_stage(k)

        @pl.when(t > HOLD)
        def _():
            first_stage(t - 1)

        @pl.when(t == HOLD + 2)
        def _():
            for k in range(HOLD):
                second_stage(k)

        @pl.when(t > HOLD + 2)
        def _():
            second_stage(t - 3)

        @pl.when(t == Z - 1)
        def _():
            for k in range(HOLD):
                third_stage(k)

        return carry

    lax.fori_loop(0, Z, step, 0)

    last = Z - 1
    core_copy(last).wait_recv()
    summed[last] = part[last, core] + got_core[last]
    for d in (6, 7, 5, 2, 3, 1, 4):
        plane_copy(d).start()
    for k in range(last - 2, last):
        second_stage(k)
    for k in range(HOLD, last):
        third_stage(k)

    for d in range(1, PLANE):
        plane_copy(d).wait_recv()
    own = summed[last, mine]
    for d in range(1, PLANE):
        own = own + got_plane[d - 1]
    for t in range(last):
        z_copy(t).wait_recv()
        own = own + got_z[t]
    sketch_ref[...] = own

    def place(at):
        return pl.ds(pl.multiple_of(at * COLS, COLS), COLS)

    both[place(col), :] = own

    def col_copy(at):
        return copy(both.at[place(at)], both.at[place(at)], col_sem.at[0], col_sem.at[1], partner)

    col_copy(col).start()
    col_copy(1 - col).wait_recv()
    gram_part[...] = lax.dot_general(
        own, both[...], (((1,), (1,)), ((), ())),
        precision=lax.Precision.HIGHEST, preferred_element_type=jnp.float32,
    ).reshape(PLANE, 8, 128)

    line = x * 2 + core

    def rs_copy(d):
        return copy(
            gram_part.at[line ^ d], got_rs.at[d - 1], rs_send.at[d - 1], rs_recv.at[d - 1], in_line(d)
        )

    for d in (4, 5, 2, 3, 6, 7, 1):
        rs_copy(d).start()
    for d in range(1, PLANE):
        rs_copy(d).wait_recv()
    piece = gram_part[line]
    for d in range(1, PLANE):
        piece = piece + got_rs[d - 1]
    me = z * 2 + y
    totals[me] = piece

    def tot_copy(k, at):
        return copy(totals.at[at], totals.at[at], tot_send.at[k - 1], tot_recv.at[k - 1], across(k))

    for k in (8, 7, 9, 6, 10, 5, 11, 4, 12, 3, 13, 2, 14, 1, 15):
        tot_copy(k, me).start()
    for k in range(1, 16):
        tot_copy(k, (me + 16 - k) % 16).wait_recv()
    piece = totals[0]
    for k in range(1, 16):
        piece = piece + totals[k]
    pieces[line] = piece * (1.0 / 16384.0)

    def out_copy(d, at):
        return copy(pieces.at[at], pieces.at[at], out_send.at[d - 1], out_recv.at[d - 1], in_line(d))

    for d in (4, 5, 2, 3, 6, 7, 1):
        out_copy(d, line).start()
    for d in range(1, PLANE):
        out_copy(d, line ^ d).wait_recv()
    gram_ref[...] = pieces[...].reshape(COLS, 128)

    def drain(t, carry):
        core_copy(t).wait_send()
        return carry

    def drain_stages(t, carry):
        @pl.when(core == 0)
        def _():
            for d in range(1, 4):
                x_first(t, d).wait_send()
            y_second(t).wait_send()

        @pl.when(core == 1)
        def _():
            y_first(t).wait_send()
            for d in range(1, 4):
                x_second(t, d).wait_send()

        z_copy(t).wait_send()
        return carry

    lax.fori_loop(0, Z, drain, 0)
    lax.fori_loop(0, last, drain_stages, 0)
    col_copy(col).wait_send()
    for d in range(1, PLANE):
        plane_copy(d).wait_send()
        rs_copy(d).wait_send()
        out_copy(d, line).wait_send()
    for k in range(1, 16):
        tot_copy(k, me).wait_send()


def hand_over(sketch_ref, gram_ref, sketch_out, gram_out):
    sketch_out[...] = sketch_ref[...]
    gram_out[...] = gram_ref[...]


def body(matrix_panel, row_signs, sample_rows):
    vmem = pl.BlockSpec(memory_space=pltpu.VMEM)
    f32 = jnp.float32
    block = (COLS, BLOCK)
    sems = pltpu.SemaphoreType.DMA
    outs = (jax.ShapeDtypeStruct(block, f32), jax.ShapeDtypeStruct(block, f32))
    sketch, gram = pl.pallas_call(
        kernel,
        out_shape=outs,
        in_specs=[vmem] * 3,
        out_specs=(vmem, vmem),
        scratch_shapes=[
            pltpu.VMEM((SPLIT * COLS, DEPTH), jnp.bfloat16),
            pltpu.VMEM((Z, CORES, PLANE) + block, f32),
            pltpu.VMEM((Z, PLANE) + block, f32),
            pltpu.VMEM((Z, PLANE) + block, f32),
            pltpu.VMEM((Z - 1, 6) + block, f32),
            pltpu.VMEM((Z - 1, 4) + block, f32),
            pltpu.VMEM((Z - 1, 3) + block, f32),
            pltpu.VMEM((PLANE - 1,) + block, f32),
            pltpu.VMEM((Z - 1,) + block, f32),
            pltpu.VMEM((Z - 1,) + block, f32),
            pltpu.VMEM((2 * COLS, BLOCK), f32),
            pltpu.VMEM((PLANE, 8, 128), f32),
            pltpu.VMEM((PLANE - 1, 8, 128), f32),
            pltpu.VMEM((16, 8, 128), f32),
            pltpu.VMEM((PLANE, 8, 128), f32),
            sems((Z,)), sems((Z,)),
            sems((Z - 1, 3)), sems((Z - 1, 3)),
            sems((Z - 1, 3)), sems((Z - 1, 3)),
            sems((PLANE - 1,)), sems((PLANE - 1,)),
            sems((Z - 1,)), sems((Z - 1,)),
            sems((2,)),
            sems((PLANE - 1,)), sems((PLANE - 1,)),
            sems((15,)), sems((15,)),
            sems((PLANE - 1,)), sems((PLANE - 1,)),
        ],
        compiler_params=pltpu.CompilerParams(
            collective_id=0, has_side_effects=True, vmem_limit_bytes=56 * 2**20
        ),
        cost_estimate=pl.CostEstimate(
            flops=2 * COLS * 8192 * 16384, bytes_accessed=2**21, transcendentals=0
        ),
    )(matrix_panel, row_signs.reshape(1, -1), sample_rows.reshape(1, -1))
    return pl.pallas_call(
        hand_over, out_shape=outs, in_specs=[vmem] * 2, out_specs=(vmem, vmem)
    )(sketch, gram)


def solution(mesh):
    return jax.shard_map(
        body,
        mesh=mesh,
        in_specs=(P("col", "row"), P("row"), P()),
        out_specs=(P("col", "row"), P("col", None)),
        check_vma=False,
    )
```

time: 71.6 us -> 61.6 us (0.86)
  Pallas kernels: 68.8 us -> 60.8 us
  local copies, waits for them, and re-layouts: 2 us -> 0 us
    pallas_call x1 -> x2, Pallas kernels: 68.8 us -> 60.8 us  [the longest x1 59.4 us: body(): pl.pallas_call(kernel, out_shape=outs, in_specs=[vmem] * 3, out_specs=(vm...]
    unnamed x4 -> x0, local copies, waits for them, and re-layouts: 2 us -> none
where the time goes in v2:
time: 61.6 us; the launch traced here: 61.5 us
  Pallas kernels  60.8 us (99%)
  between operations  0.64 us (1%)
    pallas_call x1, Pallas kernels, body(): pl.pallas_call(kernel, out_shape=outs, in_specs=[vmem] * 3, out_specs=(vm...  59.4 us
    pallas_call x1, Pallas kernels, body(): pl.pallas_call(hand_over, out_shape=outs, in_specs=[vmem] * 2, out_specs=...  1.4 us

profile of v2, /device:TPU:1, one launch (start us, length us, event | category | flops | bytes accessed | tf_op | source)
XLA Modules:
  0.0 61.5 jit_solution(15621845560168468125)
XLA Ops:
  0.6 59.4 %shard_map.50 = (f32[64,128]{1,0:T(8,128)}, f32[64,128]{1,0:T(8,128)}) custom-call(bf16[64,8192]{1,0:T(8,128)(2,1)} %x_ref.1, s32[1,8192]{1,0:T(1,128)} %bitcast.3, s32[1,16384]{1,0:T(1,128)} %bitcast.2), custom_call_target="tpu_custom_call" | custom-call | flops 17179869184 | bytes 2097152 | tf_op jit(solution)/shard_map/pallas_call | solution.py:364
  60.1 1.4 %shard_map.51 = (f32[64,128]{1,0:T(8,128)}, f32[64,128]{1,0:T(8,128)}) custom-call(f32[64,128]{1,0:T(8,128)} %get-tuple-element.4.sketch_ref, f32[64,128]{1,0:T(8,128)} %get-tuple-element.5.gram_ref), custom_call_target="tpu_custom_call" | custom-call | tf_op jit(solution)/shard_map/pallas_call | solution.py:402

commit v3 on v2

--- a/solution.py
+++ b/solution.py
@@ -16,7 +16,7 @@
 SPLIT = 4
 DEPTH = 2048
 CHUNK = PLANE * CORES * BLOCK
-HOLD = 2
+TWO_STEP = 6
 
 
 def parity(value, shift):
@@ -61,10 +61,10 @@
 def kernel(
     x_ref, sign_ref, rows_ref, sketch_ref, gram_ref,
     xs, part, got_core, summed, got_first, middle, got_second, got_plane, send_z, got_z,
-    both, gram_part, got_rs, totals, pieces,
-    core_send, core_recv, first_send, first_recv, second_send, second_recv,
+    got_cross, early, got_early, both, gram_part, got_rs, totals, pieces,
+    greet, core_send, core_recv, first_send, first_recv, second_send, second_recv,
     plane_send, plane_recv, z_send, z_recv,
-    col_sem, rs_send, rs_recv, tot_send, tot_recv, out_send, out_recv,
+    cross_sem, col_sem, rs_send, rs_recv, tot_send, tot_recv, out_send, out_recv,
 ):
     position = lax.axis_index("row")
     col = lax.axis_index("col")
@@ -74,8 +74,8 @@
     core = position % 2
     mine = y * 4 + x
 
-    def device(z_at=z, y_at=y, x_at=x, core_at=core):
-        return (((z_at * 2 + y_at) * 4 + x_at) * 2 + core_at, col)
+    def device(z_at=z, y_at=y, x_at=x, core_at=core, col_at=col):
+        return (((z_at * 2 + y_at) * 4 + x_at) * 2 + core_at, col_at)
 
     def in_plane(d):
         return device(y_at=y ^ (d // 4), x_at=x ^ (d % 4))
@@ -90,9 +90,9 @@
     partner = (position, 1 - col)
 
     barrier = pltpu.get_barrier_semaphore()
-    known = [in_plane(d) for d in range(1, 8)]
+    beside = [device(z_at=(z + 1) % Z), device(z_at=(z + 7) % Z)]
+    known = beside + [in_plane(d) for d in range(1, 8)]
     known += [in_line(d) for d in (1, 3, 5, 7)]
-    known += [device(z_at=(z + k) % Z, y_at=y ^ d) for k in range(1, Z) for d in range(2)]
     known += [partner]
     for to in known:
         pl.semaphore_signal(barrier, inc=1, device_id=to, device_id_type=MESH)
@@ -142,10 +142,16 @@
             second_send.at[t, d - 1], second_recv.at[t, d - 1], device(x_at=x ^ d),
         )
 
-    def plane_copy(d):
-        return copy(
-            summed.at[Z - 1, mine ^ d], got_plane.at[d - 1],
-            plane_send.at[d - 1], plane_recv.at[d - 1], in_plane(d),
+    def plane_copy(t, d):
+        return copy(
+            summed.at[t, mine ^ d], got_plane.at[t - TWO_STEP, d - 1],
+            plane_send.at[t - TWO_STEP, d - 1], plane_recv.at[t - TWO_STEP, d - 1], in_plane(d),
+        )
+
+    def cross_copy():
+        return copy(
+            send_z.at[Z - 2], got_cross, cross_sem.at[0], cross_sem.at[1],
+            device(z_at=(z + 7) % Z, col_at=1 - col),
         )
 
     def z_copy(t):
@@ -203,79 +209,100 @@
 
         z_copy(t).start()
 
+    def plane_stage(t):
+        core_copy(t).wait_recv()
+        summed[t] = part[t, core] + got_core[t]
+        for d in (6, 7, 5, 2, 3, 1, 4):
+            plane_copy(t, d).start()
+
+    def plane_sum(t):
+        for d in range(1, PLANE):
+            plane_copy(t, d).wait_recv()
+        block = summed[t, mine]
+        for d in range(1, PLANE):
+            block = block + got_plane[t - TWO_STEP, d - 1]
+        return block
+
+    def each(stage, first, end):
+        def one(k, carry):
+            stage(k)
+            return carry
+
+        lax.fori_loop(first, end, one, 0)
+
+    last = Z - 1
+    hold = jnp.where(z < 3, 2, 1)
+
     def step(t, carry):
         start = pl.multiple_of(target(t) * CHUNK, CHUNK)
         chunk = mixed_chunk(position, rows_ref[:, pl.ds(start, CHUNK)], xs)
         for j in range(16):
             part[t, j % 2, j // 2] = chunk[:, j * BLOCK:(j + 1) * BLOCK]
 
-        @pl.when(t == HOLD - 1)
+        @pl.when(t == hold - 1)
         def _():
             pl.semaphore_wait(barrier, len(known))
-            for k in range(HOLD):
-                core_copy(k).start()
-
-        @pl.when(t >= HOLD)
+            each(lambda k: core_copy(k).start(), 0, hold)
+
+        @pl.when(t >= hold)
         def _():
             core_copy(t).start()
 
-        @pl.when(t == HOLD)
-        def _():
-            for k in range(HOLD):
-                first_stage(k)
-
-        @pl.when(t > HOLD)
-        def _():
-            first_stage(t - 1)
-
-        @pl.when(t == HOLD + 2)
-        def _():
-            for k in range(HOLD):
-                second_stage(k)
-
-        @pl.when(t > HOLD + 2)
-        def _():
-            second_stage(t - 3)
-
-        @pl.when(t == Z - 1)
-        def _():
-            for k in range(HOLD):
-                third_stage(k)
+        @pl.when((t >= hold) & (t < hold + 3))
+        def _():
+            pl.semaphore_wait(greet.at[t - hold], 2)
+
+        @pl.when((t >= hold - 1) & (t < hold + 2))
+        def _():
+            for to in beside:
+                pl.semaphore_signal(greet.at[t - hold + 1], inc=1, device_id=to, device_id_type=MESH)
+
+        @pl.when((t >= hold) & (t < last))
+        def _():
+            each(first_stage, jnp.where(t == hold, 0, t - 1), t)
+
+        @pl.when(t == last)
+        def _():
+            plane_stage(last - 1)
+
+        @pl.when(t >= 5)
+        def _():
+            each(second_stage, 2 * (t - 5), jnp.minimum(2 * (t - 5) + 2, 5))
+
+        @pl.when(t == last)
+        def _():
+            each(third_stage, 0, 2)
 
         return carry
 
     lax.fori_loop(0, Z, step, 0)
 
-    last = Z - 1
-    core_copy(last).wait_recv()
-    summed[last] = part[last, core] + got_core[last]
-    for d in (6, 7, 5, 2, 3, 1, 4):
-        plane_copy(d).start()
-    for k in range(last - 2, last):
-        second_stage(k)
-    for k in range(HOLD, last):
-        third_stage(k)
-
-    for d in range(1, PLANE):
-        plane_copy(d).wait_recv()
-    own = summed[last, mine]
-    for d in range(1, PLANE):
-        own = own + got_plane[d - 1]
-    for t in range(last):
+    plane_stage(last)
+    second_stage(5)
+    each(third_stage, 2, TWO_STEP)
+    send_z[last - 1] = plane_sum(last - 1)
+    z_copy(last - 1).start()
+    cross_copy().start()
+    own = plane_sum(last)
+    for t in range(last - 1):
         z_copy(t).wait_recv()
         own = own + got_z[t]
-    sketch_ref[...] = own
+    early[...] = own
 
     def place(at):
         return pl.ds(pl.multiple_of(at * COLS, COLS), COLS)
 
+    def col_copy():
+        return copy(early, got_early, col_sem.at[0], col_sem.at[1], partner)
+
+    col_copy().start()
+    z_copy(last - 1).wait_recv()
+    own = own + got_z[last - 1]
+    sketch_ref[...] = own
     both[place(col), :] = own
-
-    def col_copy(at):
-        return copy(both.at[place(at)], both.at[place(at)], col_sem.at[0], col_sem.at[1], partner)
-
-    col_copy(col).start()
-    col_copy(1 - col).wait_recv()
+    cross_copy().wait_recv()
+    col_copy().wait_recv()
+    both[place(1 - col), :] = got_early[...] + got_cross[...]
     gram_part[...] = lax.dot_general(
         own, both[...], (((1,), (1,)), ((), ())),
         precision=lax.Precision.HIGHEST, preferred_element_type=jnp.float32,
@@ -340,10 +367,13 @@
         return carry
 
     lax.fori_loop(0, Z, drain, 0)
-    lax.fori_loop(0, last, drain_stages, 0)
-    col_copy(col).wait_send()
+    lax.fori_loop(0, TWO_STEP, drain_stages, 0)
+    z_copy(last - 1).wait_send()
+    cross_copy().wait_send()
+    col_copy().wait_send()
     for d in range(1, PLANE):
-        plane_copy(d).wait_send()
+        plane_copy(last - 1, d).wait_send()
+        plane_copy(last, d).wait_send()
         rs_copy(d).wait_send()
         out_copy(d, line).wait_send()
     for k in range(1, 16):
@@ -371,23 +401,27 @@
             pltpu.VMEM((Z, CORES, PLANE) + block, f32),
             pltpu.VMEM((Z, PLANE) + block, f32),
             pltpu.VMEM((Z, PLANE) + block, f32),
-            pltpu.VMEM((Z - 1, 6) + block, f32),
-            pltpu.VMEM((Z - 1, 4) + block, f32),
-            pltpu.VMEM((Z - 1, 3) + block, f32),
-            pltpu.VMEM((PLANE - 1,) + block, f32),
+            pltpu.VMEM((TWO_STEP, 6) + block, f32),
+            pltpu.VMEM((TWO_STEP, 4) + block, f32),
+            pltpu.VMEM((TWO_STEP, 3) + block, f32),
+            pltpu.VMEM((Z - TWO_STEP, PLANE - 1) + block, f32),
             pltpu.VMEM((Z - 1,) + block, f32),
             pltpu.VMEM((Z - 1,) + block, f32),
+            pltpu.VMEM(block, f32),
+            pltpu.VMEM(block, f32),
+            pltpu.VMEM(block, f32),
             pltpu.VMEM((2 * COLS, BLOCK), f32),
             pltpu.VMEM((PLANE, 8, 128), f32),
             pltpu.VMEM((PLANE - 1, 8, 128), f32),
             pltpu.VMEM((16, 8, 128), f32),
             pltpu.VMEM((PLANE, 8, 128), f32),
+            pltpu.SemaphoreType.REGULAR((3,)),
             sems((Z,)), sems((Z,)),
-            sems((Z - 1, 3)), sems((Z - 1, 3)),
-            sems((Z - 1, 3)), sems((Z - 1, 3)),
-            sems((PLANE - 1,)), sems((PLANE - 1,)),
+            sems((TWO_STEP, 3)), sems((TWO_STEP, 3)),
+            sems((TWO_STEP, 3)), sems((TWO_STEP, 3)),
+            sems((Z - TWO_STEP, PLANE - 1)), sems((Z - TWO_STEP, PLANE - 1)),
             sems((Z - 1,)), sems((Z - 1,)),
-            sems((2,)),
+            sems((2,)), sems((2,)),
             sems((PLANE - 1,)), sems((PLANE - 1,)),
             sems((15,)), sems((15,)),
             sems((PLANE - 1,)), sems((PLANE - 1,)),

time: 61.6 us -> 61 us (level)
    pallas_call x1, Pallas kernels: 59.4 us -> 58.7 us  [body(): pl.pallas_call(kernel, out_shape=outs, in_specs=[vmem] * 3, out_specs=(vm...]
where the time goes in v3:
time: 61 us; the launch traced here: 60.8 us
  Pallas kernels  60.2 us (99%)
  between operations  0.64 us (1%)
    pallas_call x1, Pallas kernels, body(): pl.pallas_call(kernel, out_shape=outs, in_specs=[vmem] * 3, out_specs=(vm...  58.7 us
    pallas_call x1, Pallas kernels, body(): pl.pallas_call(hand_over, out_shape=outs, in_specs=[vmem] * 2, out_specs=...  1.4 us

profile of v3, /device:TPU:1, one launch (start us, length us, event | category | flops | bytes accessed | tf_op | source)
XLA Modules:
  0.0 60.8 jit_solution(10276457526009220643)
XLA Ops:
  0.6 58.7 %shard_map.50 = (f32[64,128]{1,0:T(8,128)}, f32[64,128]{1,0:T(8,128)}) custom-call(bf16[64,8192]{1,0:T(8,128)(2,1)} %x_ref.1, s32[1,8192]{1,0:T(1,128)} %bitcast.3, s32[1,16384]{1,0:T(1,128)} %bitcast.2), custom_call_target="tpu_custom_call" | custom-call | flops 17179869184 | bytes 2097152 | tf_op jit(solution)/shard_map/pallas_call | solution.py:394
  59.4 1.4 %shard_map.51 = (f32[64,128]{1,0:T(8,128)}, f32[64,128]{1,0:T(8,128)}) custom-call(f32[64,128]{1,0:T(8,128)} %get-tuple-element.4.sketch_ref, f32[64,128]{1,0:T(8,128)} %get-tuple-element.5.gram_ref), custom_call_target="tpu_custom_call" | custom-call | tf_op jit(solution)/shard_map/pallas_call | solution.py:436

commit v4 on v3

--- a/solution.py
+++ b/solution.py
@@ -16,7 +16,7 @@
 SPLIT = 4
 DEPTH = 2048
 CHUNK = PLANE * CORES * BLOCK
-TWO_STEP = 6
+TWO_STEP = 5
 
 
 def parity(value, shift):
@@ -118,6 +118,13 @@
             device(core_at=1 - core),
         )
 
+    def half_copy(half):
+        blocks = pl.ds(4 * half, 4)
+        return copy(
+            part.at[Z - 1, 1 - core, blocks], got_core.at[Z - 1, blocks],
+            core_send.at[Z - 1 + half], core_recv.at[Z - 1 + half], device(core_at=1 - core),
+        )
+
     def x_first(t, d):
         return copy(
             summed.at[t, pl.ds(2 * (x ^ d), 2)], got_first.at[t, pl.ds(2 * (d - 1), 2)],
@@ -215,6 +222,21 @@
         for d in (6, 7, 5, 2, 3, 1, 4):
             plane_copy(t, d).start()
 
+    def half_stage(half):
+        half_copy(half).wait_recv()
+        blocks = pl.ds(4 * half, 4)
+        summed[last, blocks] = part[last, core, blocks] + got_core[last, blocks]
+
+        @pl.when(y == half)
+        def _():
+            for d in (2, 3, 1):
+                plane_copy(last, d).start()
+
+        @pl.when(y != half)
+        def _():
+            for d in (6, 7, 5, 4):
+                plane_copy(last, d).start()
+
     def plane_sum(t):
         for d in range(1, PLANE):
             plane_copy(t, d).wait_recv()
@@ -231,57 +253,68 @@
         lax.fori_loop(first, end, one, 0)
 
     last = Z - 1
-    hold = jnp.where(z < 3, 2, 1)
+
+    def rows_at(t, begin, count):
+        start = pl.multiple_of(target(t) * CHUNK + begin, count)
+        return rows_ref[:, pl.ds(start, count)]
 
     def step(t, carry):
-        start = pl.multiple_of(target(t) * CHUNK, CHUNK)
-        chunk = mixed_chunk(position, rows_ref[:, pl.ds(start, CHUNK)], xs)
+        chunk = mixed_chunk(position, rows_at(t, 0, CHUNK), xs)
         for j in range(16):
             part[t, j % 2, j // 2] = chunk[:, j * BLOCK:(j + 1) * BLOCK]
 
-        @pl.when(t == hold - 1)
+        @pl.when(t == 0)
         def _():
             pl.semaphore_wait(barrier, len(known))
-            each(lambda k: core_copy(k).start(), 0, hold)
-
-        @pl.when(t >= hold)
-        def _():
-            core_copy(t).start()
-
-        @pl.when((t >= hold) & (t < hold + 3))
-        def _():
-            pl.semaphore_wait(greet.at[t - hold], 2)
-
-        @pl.when((t >= hold - 1) & (t < hold + 2))
+
+        core_copy(t).start()
+
+        @pl.when((t >= 1) & (t < 4))
+        def _():
+            pl.semaphore_wait(greet.at[t - 1], 2)
+
+        @pl.when(t < 3)
         def _():
             for to in beside:
-                pl.semaphore_signal(greet.at[t - hold + 1], inc=1, device_id=to, device_id_type=MESH)
-
-        @pl.when((t >= hold) & (t < last))
-        def _():
-            each(first_stage, jnp.where(t == hold, 0, t - 1), t)
-
-        @pl.when(t == last)
-        def _():
+                pl.semaphore_signal(greet.at[t], inc=1, device_id=to, device_id_type=MESH)
+
+        @pl.when((t >= 1) & (t <= TWO_STEP))
+        def _():
+            first_stage(t - 1)
+
+        @pl.when(t > TWO_STEP)
+        def _():
+            plane_stage(t - 1)
+
+        @pl.when(t >= 3)
+        def _():
+            second_stage(t - 3)
+
+        @pl.when(t >= 5)
+        def _():
+            third_stage(t - 5)
+
+        return carry
+
+    lax.fori_loop(0, last, step, 0)
+
+    for half in range(2):
+        chunk = mixed_chunk(position, rows_at(last, half * CHUNK // 2, CHUNK // 2), xs)
+        for j in range(8):
+            part[last, j % 2, 4 * half + j // 2] = chunk[:, j * BLOCK:(j + 1) * BLOCK]
+        half_copy(half).start()
+        if half == 0:
             plane_stage(last - 1)
-
-        @pl.when(t >= 5)
-        def _():
-            each(second_stage, 2 * (t - 5), jnp.minimum(2 * (t - 5) + 2, 5))
-
-        @pl.when(t == last)
-        def _():
-            each(third_stage, 0, 2)
-
-        return carry
-
-    lax.fori_loop(0, Z, step, 0)
-
-    plane_stage(last)
-    second_stage(5)
-    each(third_stage, 2, TWO_STEP)
-    send_z[last - 1] = plane_sum(last - 1)
-    z_copy(last - 1).start()
+            each(second_stage, 4, TWO_STEP)
+            third_stage(2)
+        else:
+            half_stage(0)
+            half_stage(1)
+
+    each(third_stage, 3, TWO_STEP)
+    for t in range(TWO_STEP, last):
+        send_z[t] = plane_sum(t)
+        z_copy(t).start()
     cross_copy().start()
     own = plane_sum(last)
     for t in range(last - 1):
@@ -366,14 +399,17 @@
         z_copy(t).wait_send()
         return carry
 
-    lax.fori_loop(0, Z, drain, 0)
+    lax.fori_loop(0, last, drain, 0)
+    half_copy(0).wait_send()
+    half_copy(1).wait_send()
     lax.fori_loop(0, TWO_STEP, drain_stages, 0)
-    z_copy(last - 1).wait_send()
+    for t in range(TWO_STEP, last):
+        z_copy(t).wait_send()
     cross_copy().wait_send()
     col_copy().wait_send()
     for d in range(1, PLANE):
-        plane_copy(last - 1, d).wait_send()
-        plane_copy(last, d).wait_send()
+        for t in range(TWO_STEP, Z):
+            plane_copy(t, d).wait_send()
         rs_copy(d).wait_send()
         out_copy(d, line).wait_send()
     for k in range(1, 16):
@@ -416,7 +452,7 @@
             pltpu.VMEM((16, 8, 128), f32),
             pltpu.VMEM((PLANE, 8, 128), f32),
             pltpu.SemaphoreType.REGULAR((3,)),
-            sems((Z,)), sems((Z,)),
+            sems((Z + 1,)), sems((Z + 1,)),
             sems((TWO_STEP, 3)), sems((TWO_STEP, 3)),
             sems((TWO_STEP, 3)), sems((TWO_STEP, 3)),
             sems((Z - TWO_STEP, PLANE - 1)), sems((Z - TWO_STEP, PLANE - 1)),

time: 61 us -> 59.7 us (0.979)
  Pallas kernels: 60.2 us -> 58.8 us
    pallas_call x1, Pallas kernels: 58.7 us -> 57.4 us  [body(): pl.pallas_call(kernel, out_shape=outs, in_specs=[vmem] * 3, out_specs=(vm...]
where the time goes in v4:
time: 59.7 us; the launch traced here: 59.5 us
  Pallas kernels  58.8 us (98%)
  between operations  0.64 us (1%)
    pallas_call x1, Pallas kernels, body(): pl.pallas_call(kernel, out_shape=outs, in_specs=[vmem] * 3, out_specs=(vm...  57.4 us
    pallas_call x1, Pallas kernels, body(): pl.pallas_call(hand_over, out_shape=outs, in_specs=[vmem] * 2, out_specs=...  1.4 us

profile of v4, /device:TPU:1, one launch (start us, length us, event | category | flops | bytes accessed | tf_op | source)
XLA Modules:
  0.0 59.5 jit_solution(6435504323795826539)
XLA Ops:
  0.6 57.4 %shard_map.50 = (f32[64,128]{1,0:T(8,128)}, f32[64,128]{1,0:T(8,128)}) custom-call(bf16[64,8192]{1,0:T(8,128)(2,1)} %x_ref.1, s32[1,8192]{1,0:T(1,128)} %bitcast.3, s32[1,16384]{1,0:T(1,128)} %bitcast.2), custom_call_target="tpu_custom_call" | custom-call | flops 17179869184 | bytes 2097152 | tf_op jit(solution)/shard_map/pallas_call | solution.py:430
  58.1 1.4 %shard_map.51 = (f32[64,128]{1,0:T(8,128)}, f32[64,128]{1,0:T(8,128)}) custom-call(f32[64,128]{1,0:T(8,128)} %get-tuple-element.4.sketch_ref, f32[64,128]{1,0:T(8,128)} %get-tuple-element.5.gram_ref), custom_call_target="tpu_custom_call" | custom-call | tf_op jit(solution)/shard_map/pallas_call | solution.py:472

commit v5 on v4

--- a/solution.py
+++ b/solution.py
@@ -16,7 +16,7 @@
 SPLIT = 4
 DEPTH = 2048
 CHUNK = PLANE * CORES * BLOCK
-TWO_STEP = 5
+TWO_STEP = 6
 
 
 def parity(value, shift):
@@ -99,9 +99,8 @@
 
     for a in range(SPLIT):
         window = slice(a * DEPTH, (a + 1) * DEPTH)
-        xs[a * COLS:(a + 1) * COLS, :] = (
-            x_ref[:, window].astype(jnp.float32) * sign_ref[:, window].astype(jnp.float32)
-        ).astype(jnp.bfloat16)
+        signs = sign_ref[:, window].astype(jnp.float32).astype(jnp.bfloat16)
+        xs[a * COLS:(a + 1) * COLS, :] = x_ref[:, window] * signs
 
     def copy(src, dst, send, recv, to):
         return pltpu.make_async_remote_copy(
@@ -305,9 +304,10 @@
         half_copy(half).start()
         if half == 0:
             plane_stage(last - 1)
-            each(second_stage, 4, TWO_STEP)
+            second_stage(4)
             third_stage(2)
         else:
+            second_stage(5)
             half_stage(0)
             half_stage(1)
 
@@ -363,22 +363,6 @@
 
     for k in (8, 7, 9, 6, 10, 5, 11, 4, 12, 3, 13, 2, 14, 1, 15):
         tot_copy(k, me).start()
-    for k in range(1, 16):
-        tot_copy(k, (me + 16 - k) % 16).wait_recv()
-    piece = totals[0]
-    for k in range(1, 16):
-        piece = piece + totals[k]
-    pieces[line] = piece * (1.0 / 16384.0)
-
-    def out_copy(d, at):
-        return copy(pieces.at[at], pieces.at[at], out_send.at[d - 1], out_recv.at[d - 1], in_line(d))
-
-    for d in (4, 5, 2, 3, 6, 7, 1):
-        out_copy(d, line).start()
-    for d in range(1, PLANE):
-        out_copy(d, line ^ d).wait_recv()
-    gram_ref[...] = pieces[...].reshape(COLS, 128)
-
     def drain(t, carry):
         core_copy(t).wait_send()
         return carry
@@ -396,14 +380,13 @@
             for d in range(1, 4):
                 x_second(t, d).wait_send()
 
-        z_copy(t).wait_send()
         return carry
 
     lax.fori_loop(0, last, drain, 0)
+    lax.fori_loop(0, TWO_STEP, drain_stages, 0)
     half_copy(0).wait_send()
     half_copy(1).wait_send()
-    lax.fori_loop(0, TWO_STEP, drain_stages, 0)
-    for t in range(TWO_STEP, last):
+    for t in range(last):
         z_copy(t).wait_send()
     cross_copy().wait_send()
     col_copy().wait_send()
@@ -411,9 +394,26 @@
         for t in range(TWO_STEP, Z):
             plane_copy(t, d).wait_send()
         rs_copy(d).wait_send()
-        out_copy(d, line).wait_send()
+
+    for k in range(1, 16):
+        tot_copy(k, (me + 16 - k) % 16).wait_recv()
+    piece = totals[0]
+    for k in range(1, 16):
+        piece = piece + totals[k]
+    pieces[line] = piece * (1.0 / 16384.0)
+
+    def out_copy(d, at):
+        return copy(pieces.at[at], pieces.at[at], out_send.at[d - 1], out_recv.at[d - 1], in_line(d))
+
+    for d in (4, 5, 2, 3, 6, 7, 1):
+        out_copy(d, line).start()
     for k in range(1, 16):
         tot_copy(k, me).wait_send()
+    for d in range(1, PLANE):
+        out_copy(d, line ^ d).wait_recv()
+    gram_ref[...] = pieces[...].reshape(COLS, 128)
+    for d in range(1, PLANE):
+        out_copy(d, line).wait_send()
 
 
 def hand_over(sketch_ref, gram_ref, sketch_out, gram_out):

time: 59.7 us -> 59 us (0.988)
  Pallas kernels: 58.8 us -> 58.2 us
    pallas_call x1, Pallas kernels: 57.4 us -> 56.8 us  [body(): pl.pallas_call(kernel, out_shape=outs, in_specs=[vmem] * 3, out_specs=(vm...]
where the time goes in v5:
time: 59 us; the launch traced here: 58.9 us
  Pallas kernels  58.2 us (99%)
  between operations  0.64 us (1%)
    pallas_call x1, Pallas kernels, body(): pl.pallas_call(kernel, out_shape=outs, in_specs=[vmem] * 3, out_specs=(vm...  56.8 us
    pallas_call x1, Pallas kernels, body(): pl.pallas_call(hand_over, out_shape=outs, in_specs=[vmem] * 2, out_specs=...  1.4 us

profile of v5, /device:TPU:1, one launch (start us, length us, event | category | flops | bytes accessed | tf_op | source)
XLA Modules:
  0.0 58.9 jit_solution(4037203909364246991)
XLA Ops:
  0.6 56.8 %shard_map.50 = (f32[64,128]{1,0:T(8,128)}, f32[64,128]{1,0:T(8,128)}) custom-call(bf16[64,8192]{1,0:T(8,128)(2,1)} %x_ref.1, s32[1,8192]{1,0:T(1,128)} %bitcast.3, s32[1,16384]{1,0:T(1,128)} %bitcast.2), custom_call_target="tpu_custom_call" | custom-call | flops 17179869184 | bytes 2097152 | tf_op jit(solution)/shard_map/pallas_call | solution.py:430
  57.5 1.4 %shard_map.51 = (f32[64,128]{1,0:T(8,128)}, f32[64,128]{1,0:T(8,128)}) custom-call(f32[64,128]{1,0:T(8,128)} %get-tuple-element.4.sketch_ref, f32[64,128]{1,0:T(8,128)} %get-tuple-element.5.gram_ref), custom_call_target="tpu_custom_call" | custom-call | tf_op jit(solution)/shard_map/pallas_call | solution.py:472

commit v6 on v5

--- a/solution.py
+++ b/solution.py
@@ -64,7 +64,7 @@
     got_cross, early, got_early, both, gram_part, got_rs, totals, pieces,
     greet, core_send, core_recv, first_send, first_recv, second_send, second_recv,
     plane_send, plane_recv, z_send, z_recv,
-    cross_sem, col_sem, rs_send, rs_recv, tot_send, tot_recv, out_send, out_recv,
+    cross_send, cross_recv, col_sem, rs_send, rs_recv, tot_send, tot_recv, out_send, out_recv,
 ):
     position = lax.axis_index("row")
     col = lax.axis_index("col")
@@ -154,10 +154,11 @@
             plane_send.at[t - TWO_STEP, d - 1], plane_recv.at[t - TWO_STEP, d - 1], in_plane(d),
         )
 
-    def cross_copy():
-        return copy(
-            send_z.at[Z - 2], got_cross, cross_sem.at[0], cross_sem.at[1],
-            device(z_at=(z + 7) % Z, col_at=1 - col),
+    def cross_copy(t):
+        at = t - (Z - 3)
+        return copy(
+            send_z.at[t], got_cross.at[at], cross_send.at[at], cross_recv.at[at],
+            device(z_at=target(t), col_at=1 - col),
         )
 
     def z_copy(t):
@@ -312,12 +313,13 @@
             half_stage(1)
 
     each(third_stage, 3, TWO_STEP)
+    cross_copy(last - 2).start()
     for t in range(TWO_STEP, last):
         send_z[t] = plane_sum(t)
         z_copy(t).start()
-    cross_copy().start()
+    cross_copy(last - 1).start()
     own = plane_sum(last)
-    for t in range(last - 1):
+    for t in range(last - 2):
         z_copy(t).wait_recv()
         own = own + got_z[t]
     early[...] = own
@@ -329,13 +331,15 @@
         return copy(early, got_early, col_sem.at[0], col_sem.at[1], partner)
 
     col_copy().start()
-    z_copy(last - 1).wait_recv()
-    own = own + got_z[last - 1]
+    for t in range(last - 2, last):
+        z_copy(t).wait_recv()
+        own = own + got_z[t]
     sketch_ref[...] = own
     both[place(col), :] = own
-    cross_copy().wait_recv()
+    cross_copy(last - 2).wait_recv()
+    cross_copy(last - 1).wait_recv()
     col_copy().wait_recv()
-    both[place(1 - col), :] = got_early[...] + got_cross[...]
+    both[place(1 - col), :] = (got_early[...] + got_cross[0]) + got_cross[1]
     gram_part[...] = lax.dot_general(
         own, both[...], (((1,), (1,)), ((), ())),
         precision=lax.Precision.HIGHEST, preferred_element_type=jnp.float32,
@@ -388,7 +392,8 @@
     half_copy(1).wait_send()
     for t in range(last):
         z_copy(t).wait_send()
-    cross_copy().wait_send()
+    cross_copy(last - 2).wait_send()
+    cross_copy(last - 1).wait_send()
     col_copy().wait_send()
     for d in range(1, PLANE):
         for t in range(TWO_STEP, Z):
@@ -443,7 +448,7 @@
             pltpu.VMEM((Z - TWO_STEP, PLANE - 1) + block, f32),
             pltpu.VMEM((Z - 1,) + block, f32),
             pltpu.VMEM((Z - 1,) + block, f32),
-            pltpu.VMEM(block, f32),
+            pltpu.VMEM((2,) + block, f32),
             pltpu.VMEM(block, f32),
             pltpu.VMEM(block, f32),
             pltpu.VMEM((2 * COLS, BLOCK), f32),
@@ -457,7 +462,7 @@
             sems((TWO_STEP, 3)), sems((TWO_STEP, 3)),
             sems((Z - TWO_STEP, PLANE - 1)), sems((Z - TWO_STEP, PLANE - 1)),
             sems((Z - 1,)), sems((Z - 1,)),
-            sems((2,)), sems((2,)),
+            sems((2,)), sems((2,)), sems((2,)),
             sems((PLANE - 1,)), sems((PLANE - 1,)),
             sems((15,)), sems((15,)),
             sems((PLANE - 1,)), sems((PLANE - 1,)),

time: 59 us -> 59.5 us (level)
  no operation moved by 1% of the time
where the time goes in v6:
time: 59.5 us; the launch traced here: 59.3 us
  Pallas kernels  58.7 us (99%)
  between operations  0.64 us (1%)
    pallas_call x1, Pallas kernels, body(): pl.pallas_call(kernel, out_shape=outs, in_specs=[vmem] * 3, out_specs=(vm...  57.3 us
    pallas_call x1, Pallas kernels, body(): pl.pallas_call(hand_over, out_shape=outs, in_specs=[vmem] * 2, out_specs=...  1.4 us

profile of v6, /device:TPU:1, one launch (start us, length us, event | category | flops | bytes accessed | tf_op | source)
XLA Modules:
  0.0 59.3 jit_solution(12076625476064922783)
XLA Ops:
  0.6 57.3 %shard_map.50 = (f32[64,128]{1,0:T(8,128)}, f32[64,128]{1,0:T(8,128)}) custom-call(bf16[64,8192]{1,0:T(8,128)(2,1)} %x_ref.1, s32[1,8192]{1,0:T(1,128)} %bitcast.3, s32[1,16384]{1,0:T(1,128)} %bitcast.2), custom_call_target="tpu_custom_call" | custom-call | flops 17179869184 | bytes 2097152 | tf_op jit(solution)/shard_map/pallas_call | solution.py:435
  57.9 1.4 %shard_map.51 = (f32[64,128]{1,0:T(8,128)}, f32[64,128]{1,0:T(8,128)}) custom-call(f32[64,128]{1,0:T(8,128)} %get-tuple-element.4.sketch_ref, f32[64,128]{1,0:T(8,128)} %get-tuple-element.5.gram_ref), custom_call_target="tpu_custom_call" | custom-call | tf_op jit(solution)/shard_map/pallas_call | solution.py:477
